TPU v7x, 128 devices: a whole 4x4x4 slice. The times are simulated.
128 devices in a mesh: doc: 8 (over x, y_hi), param: 16 (over z, y_lo, core).
Axes of the slice: x: 4, y: 4 (y_hi: 2, y_lo: 2; y = y_hi * 2 + y_lo), z: 4, core: 2. Of those that a mesh axis runs over, the one named last changes fastest.
Arguments:
- activations: bfloat16 [512, 128, 13824], P('doc', None, 'param'), may hold values from -6 to 6
- out_grads: bfloat16 [512, 128, 5120], P('doc', None, 'param'), may hold values from -6 to 6
- proj_in: bfloat16 [64, 13824], P(None, 'param'), may hold values from -0.0546875 to 0.0546875
- proj_out: bfloat16 [64, 5120], P(None, 'param'), may hold values from -0.078125 to 0.078125
- lengths: int32 [512], P('doc'), may hold values from 1 to 128, as said below
- loss_mask: int32 [512, 128], P('doc'), may hold values 0 or 1
- queries: float32 [1024, 4096], P(('doc', 'param')), may hold values from -6 to 6
- left_pre: float32 [64, 64], replicated, may hold values from -0.75 to 0.75
- right_pre: float32 [64, 64], replicated, may hold values from -0.75 to 0.75
Outputs:
- scores: float32 [512, 1024], P(('doc', 'param'))
Inputs may be any that keep to these rules, and one draw needn't show every extreme that they name: `lengths`: some document has 128 tokens and some has 1.
All inputs are finite; a program needn't handle non-finite values. No bound on the sum of `loss_mask` on one device may be relied on, other than what follows from the above.
Results may differ from a plain program's by a relative error of at most 0.0003.
Values sent between devices are 32-bit elements; how exact they have to be, the bound alone decides.
A program may use at most 128 MiB of HBM per device.

v0:
```python
import functools

import jax
import jax.numpy as jnp
from jax import lax
from jax.experimental import pallas as pl
from jax.experimental.pallas import tpu as pltpu
from jax.sharding import PartitionSpec as P

MESH = pl.DeviceIdType.MESH
F32 = jnp.float32
BF16 = jnp.bfloat16
HIGHEST = lax.Precision.HIGHEST

RANK = 64
SEQ = 128
OWNED = 4
ROWS = OWNED * SEQ
HALF_A = 144
HALF_B = 112
PART_A = 2 * HALF_A
AHEAD = 3
ORDER = ((2, 0), (2, 1), (1, 0), (1, 1), (3, 0), (3, 1), (0, 0), (0, 1))
PLACE = {step: j for j, step in enumerate(ORDER)}
PEERS = tuple(
    (dz, dy, dc) for dz in (2, 1, 3, 0) for dy in (1, 0) for dc in (1, 0) if (dz, dy, dc) != (0, 0, 0)
)
N_SEMS = 8 + 18 + 5 + 15 + 1 + 3 + 15 + 15


def iota(shape, dim):
    return lax.broadcasted_iota(jnp.int32, shape, dim)


def split(x):
    high = x.astype(BF16)
    return high, (x - high.astype(F32)).astype(BF16)


def dot(a, b, contract=(1, 0), precision=None):
    return lax.dot_general(
        a, b, (((contract[0],), (contract[1],)), ((), ())), precision=precision, preferred_element_type=F32
    )


def kernel(
    act, grad, pin, pout, lengths, mask, queries, left, right,
    out,
    act_v, grad_v, pin_v, pout_v, len_s, mask_v, q_v, left_v, right_v, w_out,
    blocks, twin, f_a, n_a, f_b, n_b, y_a, y_b,
    t_own, t_all, t_high, t_low, g_own, g_all, s_own, s_all,
    load_sem, small_sem, send_sem, recv_sem,
):
    doc, me = lax.axis_index("doc"), lax.axis_index("param")
    x, hi = doc // 2, lax.rem(doc, 2)
    z, lo, core = me // 4, lax.rem(me // 2, 2), lax.rem(me, 2)

    def place(dz, dy, dc):
        py = 1 - lo if dy else lo
        pc = 1 - core if dc else core
        return lax.rem(z + dz, 4) * 4 + py * 2 + pc

    def part(param):
        pz, py, pc = param // 4, lax.rem(param // 2, 2), lax.rem(param, 2)
        return pz * 4 + (py + hi - 2 * py * hi) * 2 + pc

    def loads(j):
        dz, own = ORDER[j]
        found = []
        for r in (1, 0):
            first = place(dz, 1 - own, r) * OWNED
            found.append(pltpu.make_async_copy(act.at[pl.ds(first, OWNED)], act_v.at[j, r], load_sem.at[j, r, 0]))
            found.append(pltpu.make_async_copy(grad.at[pl.ds(first, OWNED)], grad_v.at[j, r], load_sem.at[j, r, 1]))
        return found

    small = [
        pltpu.make_async_copy(src, dst, small_sem.at[i])
        for i, (src, dst) in enumerate(
            (
                (pin, pin_v), (pout, pout_v), (queries, q_v), (left, left_v), (right, right_v),
                (mask, mask_v), (lengths, len_s),
            )
        )
    ]
    small[0].start()
    small[1].start()
    for copy in loads(0):
        copy.start()
    for copy in small[2:]:
        copy.start()
    for j in range(1, AHEAD):
        for copy in loads(j):
            copy.start()

    barrier = pltpu.get_barrier_semaphore()
    greet = [(doc, place(*peer)) for peer in PEERS]
    greet += [(lax.rem(x + dx, 4) * 2 + hi, me) for dx in (1, 2, 3)]
    y_next = (x * 2 + 1 - hi, place(0, 1, 0))
    greet.append(y_next)
    for device in greet:
        pl.semaphore_signal(barrier, inc=1, device_id=device, device_id_type=MESH)

    small[0].wait()
    small[1].wait()
    r_, c_ = iota((RANK, RANK), 0), iota((RANK, RANK), 1)
    odd = (r_ >= 32).astype(jnp.int32)
    pick = jnp.where(c_ == 2 * (r_ - 32 * odd) + odd, 1.0, 0.0).astype(BF16)
    w_out[...] = dot(pick, pout_v[...]).astype(BF16)

    counter = [0]
    sent = []

    def send(src, dst, device):
        i = counter[0]
        counter[0] += 1
        copy = pltpu.make_async_remote_copy(
            src_ref=src, dst_ref=dst, send_sem=send_sem.at[i], recv_sem=recv_sem.at[i],
            device_id=device, device_id_type=MESH,
        )
        copy.start()
        sent.append(copy)
        return copy

    up, down = (doc, place(1, 0, 0)), (doc, place(3, 0, 0))
    twin_id, y_id = (doc, place(0, 0, 1)), (doc, place(0, 1, 0))
    core_copy, y_copy, z_copy = {}, {}, {}

    def project(j):
        for copy in loads(j):
            copy.wait()

        def one(i, carry):
            r = 1 - i
            a = jnp.concatenate([act_v[j, r, d] for d in range(OWNED)], axis=1)
            g = jnp.concatenate([grad_v[j, r, d] for d in range(OWNED)], axis=1)
            o_rows, i_rows = dot(w_out[...], g), dot(pin_v[...], a)
            for d in range(OWNED):
                blocks[j, r, d * SEQ : d * SEQ + RANK] = o_rows[:, d * SEQ : (d + 1) * SEQ]
                blocks[j, r, d * SEQ + RANK : (d + 1) * SEQ] = i_rows[:, d * SEQ : (d + 1) * SEQ]
            return carry

        lax.fori_loop(0, 2, one, 0)
        core_copy[j] = send(blocks.at[j, 1], twin.at[j], twin_id)

    def ref(t, dz, half):
        if t < 2:
            return blocks.at[PLACE[dz, t], 0, pl.ds(half * HALF_A, HALF_A)]
        return blocks.at[PLACE[dz, 1], 0, pl.ds(PART_A + half * HALF_B, HALF_B)]

    def far(t, half):
        return f_a.at[t, half] if t < 2 else f_b.at[half]

    def near(t, side, half):
        return n_a.at[t, side, half] if t < 2 else n_b.at[side, half]

    def send_far(t):
        z_copy[t, "f0"] = send(ref(t, 2, 0), far(t, 0), up)
        z_copy[t, "f1"] = send(ref(t, 2, 1), far(t, 1), down)

    def send_up_now(t):
        z_copy[t, "u1"] = send(ref(t, 1, 1), near(t, 0, 1), up)

    def send_down_now(t):
        z_copy[t, "d0"] = send(ref(t, 3, 0), near(t, 1, 0), down)

    def send_up_sum(t):
        z_copy[t, "f0"].wait_recv()
        ref(t, 1, 0)[...] += far(t, 0)[...]
        z_copy[t, "u0"] = send(ref(t, 1, 0), near(t, 0, 0), up)

    def send_down_sum(t):
        z_copy[t, "f1"].wait_recv()
        ref(t, 3, 1)[...] += far(t, 1)[...]
        z_copy[t, "d1"] = send(ref(t, 3, 1), near(t, 1, 1), down)

    def finish(t):
        for name in ("u1", "d0", "u0", "d1"):
            z_copy[t, name].wait_recv()
        for half in (0, 1):
            ref(t, 0, half)[...] += near(t, 0, half)[...] + near(t, 1, half)[...]

    def collect(j):
        dz, own = ORDER[j]
        core_copy[j].wait_recv()
        blocks[j, 0] += twin[j]
        if not own:
            y_copy[dz] = send(blocks.at[j, 0, pl.ds(PART_A, ROWS - PART_A)], y_b.at[dz], y_id)
        if dz == 2:
            send_far(own)
        elif dz == 1:
            send_up_now(own)
        elif dz == 3:
            send_down_now(own)

    def y_sum(dz):
        y_copy[dz].wait_recv()
        blocks[PLACE[dz, 1], 0, PART_A:ROWS] += y_b[dz]

    def precondition():
        for copy in small[2:5]:
            copy.wait()
        for m in range(32):
            t_own[m] = q_v[:, m * 128 : (m + 1) * 128]
        wide = jnp.where(lax.rem(iota((128, RANK), 0), RANK) == iota((128, RANK), 1), 1.0, 0.0)
        same = (iota((128, 128), 0) // RANK) == (iota((128, 128), 1) // RANK)
        both = dot(dot(wide, right_v[...], precision=HIGHEST), wide, (1, 1), precision=HIGHEST)
        both = jnp.where(same, both, 0.0)
        u = dot(t_own[...].reshape(256, 128), both, precision=HIGHEST)
        row, col = iota((256, RANK), 0), iota((256, RANK), 1)
        same_q = lax.rem(iota((256, 256), 0), 8) == lax.rem(iota((256, 256), 1), 8)
        take = [jnp.where(col == 2 * (row // 8) + e, 1.0, 0.0) for e in (0, 1)]
        lane = iota((256, 128), 1)
        halves = []
        for e_out in (0, 1):
            rows = dot(take[e_out], left_v[...], precision=HIGHEST)
            pieces = []
            for e_in in (0, 1):
                a = jnp.where(same_q, dot(rows, take[e_in], (1, 1), precision=HIGHEST), 0.0)
                pieces.append(dot(a, u, precision=HIGHEST))
            halves.append(pieces)
        low = halves[0][0] + pltpu.roll(halves[0][1], RANK, 1)
        high = pltpu.roll(halves[1][0], RANK, 1) + halves[1][1]
        t_own[...] = jnp.where(lane < RANK, low, high).reshape(32, 8, 128)

    t_copy = []

    def spread_queries():
        for peer in PEERS:
            param = place(*peer)
            t_copy.append(
                send(t_own.at[pl.ds(2 * part(param), 2)], t_all.at[:, doc, me], (doc, param))
            )
        mine = part(me)
        for m in (0, 1):
            t_all[m, doc, me] = t_own[2 * mine + m]

    def spread_y():
        for copy in t_copy:
            copy.wait_recv()
        return send(t_all.at[:, doc], t_all.at[:, doc], y_next)

    def spread_x(copy):
        copy.wait_recv()
        return [
            send(t_all.at[:, pl.ds(2 * x, 2)], t_all.at[:, pl.ds(2 * x, 2)], (lax.rem(x + dx, 4) * 2 + hi, me))
            for dx in (2, 1, 3)
        ]

    def chunk(j):
        if j + AHEAD < len(ORDER):
            for copy in loads(j + AHEAD):
                copy.start()
        if j == 0:
            pl.semaphore_wait(barrier, len(greet))
        project(j)

    chunk(0)
    chunk(1)
    collect(0)
    chunk(2)
    collect(1)
    precondition()
    spread_queries()
    collect(2)
    chunk(3)
    collect(3)
    chunk(4)
    send_up_sum(0)
    collect(4)
    send_down_sum(0)
    chunk(5)
    send_up_sum(1)
    collect(5)
    send_down_sum(1)
    y_sum(2)
    send_far(2)
    t_y = spread_y()
    chunk(6)
    collect(6)
    chunk(7)
    collect(7)
    y_sum(1)
    send_up_now(2)
    y_sum(3)
    send_down_now(2)
    t_x = spread_x(t_y)
    send_up_sum(2)
    send_down_sum(2)
    finish(0)
    last = send(blocks.at[PLACE[0, 0], 0, pl.ds(0, PART_A)], y_a, y_id)
    finish(1)
    for copy in t_x:
        copy.wait_recv()
    for m in (0, 1):
        high, low = split(t_all[m].reshape(1024, 128))
        t_high[:, m * 128 : (m + 1) * 128] = high
        t_low[:, m * 128 : (m + 1) * 128] = low
    y_sum(0)
    finish(2)
    last.wait_recv()
    home = PLACE[0, 1]
    blocks[home, 0, 0:PART_A] += y_a[...]

    for copy in small[5:]:
        copy.wait()
    lane = iota((32, 128), 1)
    for d in range(OWNED):
        row = me * OWNED + d
        weight = jnp.where(iota((1, SEQ), 1) < len_s[row], mask_v[pl.ds(row, 1), :].astype(F32), 0.0)
        o_rows = blocks[home, 0, d * SEQ : d * SEQ + RANK] * weight
        i_rows = blocks[home, 0, d * SEQ + RANK : (d + 1) * SEQ]
        prod = dot(jnp.concatenate(split(o_rows), axis=0), jnp.concatenate(split(i_rows), axis=0), (1, 1))
        prod = prod[:RANK] + prod[RANK:]
        prod = prod + pltpu.roll(prod, RANK, 1)
        whole = jnp.where(lane < RANK, prod[:32], prod[32:])
        for k in range(16):
            g_own[k, 2 * d : 2 * d + 2] = whole[2 * k : 2 * k + 2]

    g_copy = []
    for peer in PEERS:
        param = place(*peer)
        g_copy.append(send(g_own.at[part(param)], g_all.at[pl.ds(pl.multiple_of(me * 8, 8), 8)], (doc, param)))
    g_all[pl.ds(pl.multiple_of(me * 8, 8), 8), :] = g_own[part(me)]
    for copy in g_copy:
        copy.wait_recv()

    docs = jnp.concatenate([g_all[pl.ds(m, 64, stride=2), :] for m in (0, 1)], axis=1)
    high, low = split(docs)
    scores = dot(jnp.concatenate([high, low], axis=0), t_high[...], (1, 1))
    scores = scores[:64] + scores[64:] + dot(high, t_low[...], (1, 1))
    scores = scores * (1.0 / (RANK * SEQ**0.5))
    for k in range(16):
        s_own[k] = scores[OWNED * k : OWNED * (k + 1)]
    s_copy = []
    for peer in PEERS:
        param = place(*peer)
        s_copy.append(send(s_own.at[param], s_all.at[me], (doc, param)))
    s_all[me] = s_own[me]
    for copy in s_copy:
        copy.wait_recv()
    total = s_all[0]
    for k in range(1, 16):
        total = total + s_all[k]
    out[...] = total
    for copy in sent:
        copy.wait_send()


def body(activations, out_grads, proj_in, proj_out, lengths, loss_mask, queries, left_pre, right_pre):
    wide_in, wide_out = activations.shape[-1], out_grads.shape[-1]
    activations, out_grads = activations.transpose(0, 2, 1), out_grads.transpose(0, 2, 1)
    vmem = pltpu.VMEM
    return pl.pallas_call(
        kernel,
        out_shape=jax.ShapeDtypeStruct((OWNED, 1024), F32),
        in_specs=[pl.BlockSpec(memory_space=pl.ANY)] * 9,
        out_specs=pl.BlockSpec(memory_space=pltpu.VMEM),
        scratch_shapes=[
            vmem((8, 2, OWNED, wide_in, SEQ), BF16),
            vmem((8, 2, OWNED, wide_out, SEQ), BF16),
            vmem(proj_in.shape, BF16),
            vmem(proj_out.shape, BF16),
            pltpu.SMEM(lengths.shape, jnp.int32),
            vmem(loss_mask.shape, jnp.int32),
            vmem(queries.shape, F32),
            vmem(left_pre.shape, F32),
            vmem(right_pre.shape, F32),
            vmem(proj_out.shape, BF16),
            vmem((8, 2, ROWS, 128), F32),
            vmem((8, ROWS, 128), F32),
            vmem((2, 2, HALF_A, 128), F32),
            vmem((2, 2, 2, HALF_A, 128), F32),
            vmem((2, HALF_B, 128), F32),
            vmem((2, 2, HALF_B, 128), F32),
            vmem((PART_A, 128), F32),
            vmem((4, ROWS - PART_A, 128), F32),
            vmem((32, 8, 128), F32),
            vmem((2, 8, 16, 8, 128), F32),
            vmem((1024, 256), BF16),
            vmem((1024, 256), BF16),
            vmem((16, 8, 128), F32),
            vmem((128, 128), F32),
            vmem((16, OWNED, 1024), F32),
            vmem((16, OWNED, 1024), F32),
            pltpu.SemaphoreType.DMA((8, 2, 2)),
            pltpu.SemaphoreType.DMA((7,)),
            pltpu.SemaphoreType.DMA((N_SEMS,)),
            pltpu.SemaphoreType.DMA((N_SEMS,)),
        ],
        compiler_params=pltpu.CompilerParams(
            collective_id=0, has_side_effects=True, vmem_limit_bytes=60 * 1024 * 1024
        ),
        cost_estimate=pl.CostEstimate(flops=1_300_000_000, bytes_accessed=20_000_000, transcendentals=0),
    )(activations, out_grads, proj_in, proj_out, lengths, loss_mask, queries, left_pre, right_pre)


def solution(mesh):
    return jax.shard_map(
        body,
        mesh=mesh,
        in_specs=(
            P("doc", None, "param"),
            P("doc", None, "param"),
            P(None, "param"),
            P(None, "param"),
            P("doc"),
            P("doc", None),
            P(("doc", "param"), None),
            P(),
            P(),
        ),
        out_specs=P(("doc", "param"), None),
        check_vma=False,
    )
```

profile of v0, /device:TPU:0, one launch (start us, length us, event | category | flops | bytes accessed | tf_op | source)
XLA Modules:
  0.0 51.8 jit_solution(14147424187526392040)
XLA Ops:
  0.0 50.4 %shard_map.91 = f32[4,1024]{1,0:T(4,128)} custom-call(bf16[64,864,128]{2,1,0:T(8,128)(2,1)} %bitcast.2, bf16[64,320,128]{2,1,0:T(8,128)(2,1)} %bitcast.3, bf16[64,864]{1,0:T(8,128)(2,1)} %pin.1, bf16[64,320]{1,0:T(8,128)(2,1)} %pout.1, s32[64]{0:T(128)} %lengths.1, s32[64,128]{1,0:T(8,128)} %mask.1, f32[8,4096]{1,0:T(8,128)} %queries.1, f32[64,64]{1,0:T(8,128)} %left.1, ...), custom_call_target="tpu_custom_call" | custom-call | flops 1300000000 | bytes 20000000 | tf_op jit(solution)/shard_map/pallas_call | solution.py:353
  50.4 1.3 %copy.11 = f32[4,1024]{1,0:T(4,128)} copy(f32[4,1024]{1,0:T(4,128)} %shard_map.91) | data formatting | bytes 32768
where the time goes:
time: 52.3 us; the launch traced here: 51.8 us
  Pallas kernels  50.4 us (96%)
  local copies, waits for them, and re-layouts  1.32 us (3%)
    pallas_call x1, Pallas kernels, body(): pl.pallas_call(kernel, out_shape=jax.ShapeDtypeStruct((OWNED, 1024), F32)...  50.4 us
    unnamed x1, local copies, waits for them, and re-layouts  1.32 us

commit v1 on v0

--- a/solution.py
+++ b/solution.py
@@ -20,12 +20,11 @@
 HALF_B = 112
 PART_A = 2 * HALF_A
 AHEAD = 3
-ORDER = ((2, 0), (2, 1), (1, 0), (1, 1), (3, 0), (3, 1), (0, 0), (0, 1))
+ORDER = ((2, 0), (2, 1), (1, 0), (3, 0), (1, 1), (3, 1), (0, 0), (0, 1))
 PLACE = {step: j for j, step in enumerate(ORDER)}
-PEERS = tuple(
-    (dz, dy, dc) for dz in (2, 1, 3, 0) for dy in (1, 0) for dc in (1, 0) if (dz, dy, dc) != (0, 0, 0)
-)
-N_SEMS = 8 + 18 + 5 + 15 + 1 + 3 + 15 + 15
+PEERS = ((2, 1), (2, 0), (1, 1), (3, 1), (1, 0), (3, 0), (0, 1))
+SLICE = 4
+N_SEMS = 8 + 18 + 5 + 7 + 2 + 4 + 3 + 7 + 7
 
 
 def iota(shape, dim):
@@ -60,9 +59,9 @@
         pc = 1 - core if dc else core
         return lax.rem(z + dz, 4) * 4 + py * 2 + pc
 
-    def part(param):
-        pz, py, pc = param // 4, lax.rem(param // 2, 2), lax.rem(param, 2)
-        return pz * 4 + (py + hi - 2 * py * hi) * 2 + pc
+    def part(dz, dy):
+        py = 1 - lo if dy else lo
+        return lax.rem(z + dz, 4) * 2 + py + hi - 2 * py * hi
 
     def loads(j):
         dz, own = ORDER[j]
@@ -82,18 +81,18 @@
             )
         )
     ]
-    small[0].start()
-    small[1].start()
+    for copy in small[:5]:
+        copy.start()
     for copy in loads(0):
         copy.start()
-    for copy in small[2:]:
+    for copy in small[5:]:
         copy.start()
     for j in range(1, AHEAD):
         for copy in loads(j):
             copy.start()
 
     barrier = pltpu.get_barrier_semaphore()
-    greet = [(doc, place(*peer)) for peer in PEERS]
+    greet = [(doc, place(*peer, 0)) for peer in PEERS] + [(doc, place(0, 0, 1))]
     greet += [(lax.rem(x + dx, 4) * 2 + hi, me) for dx in (1, 2, 3)]
     y_next = (x * 2 + 1 - hi, place(0, 1, 0))
     greet.append(y_next)
@@ -199,102 +198,105 @@
     def precondition():
         for copy in small[2:5]:
             copy.wait()
-        for m in range(32):
-            t_own[m] = q_v[:, m * 128 : (m + 1) * 128]
-        wide = jnp.where(lax.rem(iota((128, RANK), 0), RANK) == iota((128, RANK), 1), 1.0, 0.0)
-        same = (iota((128, 128), 0) // RANK) == (iota((128, 128), 1) // RANK)
-        both = dot(dot(wide, right_v[...], precision=HIGHEST), wide, (1, 1), precision=HIGHEST)
-        both = jnp.where(same, both, 0.0)
-        u = dot(t_own[...].reshape(256, 128), both, precision=HIGHEST)
-        row, col = iota((256, RANK), 0), iota((256, RANK), 1)
-        same_q = lax.rem(iota((256, 256), 0), 8) == lax.rem(iota((256, 256), 1), 8)
-        take = [jnp.where(col == 2 * (row // 8) + e, 1.0, 0.0) for e in (0, 1)]
-        lane = iota((256, 128), 1)
-        halves = []
-        for e_out in (0, 1):
-            rows = dot(take[e_out], left_v[...], precision=HIGHEST)
-            pieces = []
-            for e_in in (0, 1):
-                a = jnp.where(same_q, dot(rows, take[e_in], (1, 1), precision=HIGHEST), 0.0)
-                pieces.append(dot(a, u, precision=HIGHEST))
-            halves.append(pieces)
-        low = halves[0][0] + pltpu.roll(halves[0][1], RANK, 1)
-        high = pltpu.roll(halves[1][0], RANK, 1) + halves[1][1]
-        t_own[...] = jnp.where(lane < RANK, low, high).reshape(32, 8, 128)
-
-    t_copy = []
+        pick32 = pick.astype(F32)
+        l_perm = dot(dot(pick32, left_v[...], precision=HIGHEST), pick32, (1, 1), precision=HIGHEST)
+        none = jnp.zeros((RANK, RANK), F32)
+        r_twice = jnp.concatenate(
+            [jnp.concatenate([right_v[...], none], axis=1), jnp.concatenate([none, right_v[...]], axis=1)], axis=0
+        )
+        rows = jnp.concatenate([q_v[:, m * 128 : (m + 1) * 128] for m in range(32)], axis=0)
+        t_own[...] = dot(rows, r_twice, precision=HIGHEST).reshape(32, 8, 128)
+        lane = iota((32, 128), 1) < RANK
+
+        def pair(a, b):
+            return jnp.where(lane, a, pltpu.roll(b, RANK, 1)), jnp.where(lane, pltpu.roll(a, RANK, 1), b)
+
+        pairs = [pair(t_own[:, 2 * i], t_own[:, 2 * i + 1]) for i in range(4)]
+        cols = jnp.concatenate([jnp.concatenate(p, axis=0) for p in pairs], axis=1)
+        cols = dot(l_perm, cols, precision=HIGHEST)
+        for i in range(4):
+            a, b = pair(cols[:32, i * 128 : (i + 1) * 128], cols[32:, i * 128 : (i + 1) * 128])
+            t_own[:, 2 * i] = a
+            t_own[:, 2 * i + 1] = b
+
+    slot = me // 2
+    t_copy, t_twin = [], []
+
+    def share(first, count):
+        block = t_all.at[:, core, pl.ds(first, count)]
+        t_twin.append(send(block, block, twin_id))
 
     def spread_queries():
         for peer in PEERS:
-            param = place(*peer)
             t_copy.append(
-                send(t_own.at[pl.ds(2 * part(param), 2)], t_all.at[:, doc, me], (doc, param))
+                send(
+                    t_own.at[pl.ds(SLICE * part(*peer), SLICE)], t_all.at[:, core, doc, slot], (doc, place(*peer, 0))
+                )
             )
-        mine = part(me)
-        for m in (0, 1):
-            t_all[m, doc, me] = t_own[2 * mine + m]
+        mine = part(0, 0)
+        for m in range(SLICE):
+            t_all[m, core, doc, slot] = t_own[SLICE * mine + m]
 
     def spread_y():
         for copy in t_copy:
             copy.wait_recv()
-        return send(t_all.at[:, doc], t_all.at[:, doc], y_next)
-
-    def spread_x(copy):
-        copy.wait_recv()
-        return [
-            send(t_all.at[:, pl.ds(2 * x, 2)], t_all.at[:, pl.ds(2 * x, 2)], (lax.rem(x + dx, 4) * 2 + hi, me))
-            for dx in (2, 1, 3)
-        ]
+        t_copy.append(send(t_all.at[:, core, doc], t_all.at[:, core, doc], y_next))
+
+    def spread_x():
+        t_copy.pop().wait_recv()
+        t_copy.clear()
+        block = t_all.at[:, core, pl.ds(2 * x, 2)]
+        for dx in (2, 1, 3):
+            t_copy.append(send(block, block, (lax.rem(x + dx, 4) * 2 + hi, me)))
+        share(2 * x, 2)
+
+    def spread_twin():
+        for dx, copy in zip((1, 3, 2), (t_copy[1], t_copy[2], t_copy[0])):
+            copy.wait_recv()
+            share(2 * lax.rem(x + 4 - dx, 4), 2)
 
     def chunk(j):
         if j + AHEAD < len(ORDER):
             for copy in loads(j + AHEAD):
                 copy.start()
-        if j == 0:
-            pl.semaphore_wait(barrier, len(greet))
         project(j)
 
+    precondition()
+    pl.semaphore_wait(barrier, len(greet))
+    spread_queries()
     chunk(0)
     chunk(1)
     collect(0)
     chunk(2)
     collect(1)
-    precondition()
-    spread_queries()
+    chunk(3)
     collect(2)
-    chunk(3)
+    spread_y()
+    chunk(4)
     collect(3)
-    chunk(4)
     send_up_sum(0)
+    chunk(5)
     collect(4)
     send_down_sum(0)
-    chunk(5)
+    chunk(6)
+    collect(5)
     send_up_sum(1)
-    collect(5)
     send_down_sum(1)
+    chunk(7)
+    collect(6)
     y_sum(2)
     send_far(2)
-    t_y = spread_y()
-    chunk(6)
-    collect(6)
-    chunk(7)
     collect(7)
+    spread_x()
     y_sum(1)
     send_up_now(2)
     y_sum(3)
     send_down_now(2)
-    t_x = spread_x(t_y)
+    finish(0)
+    last = send(blocks.at[PLACE[0, 0], 0, pl.ds(0, PART_A)], y_a, y_id)
     send_up_sum(2)
     send_down_sum(2)
-    finish(0)
-    last = send(blocks.at[PLACE[0, 0], 0, pl.ds(0, PART_A)], y_a, y_id)
     finish(1)
-    for copy in t_x:
-        copy.wait_recv()
-    for m in (0, 1):
-        high, low = split(t_all[m].reshape(1024, 128))
-        t_high[:, m * 128 : (m + 1) * 128] = high
-        t_low[:, m * 128 : (m + 1) * 128] = low
     y_sum(0)
     finish(2)
     last.wait_recv()
@@ -313,33 +315,42 @@
         prod = prod[:RANK] + prod[RANK:]
         prod = prod + pltpu.roll(prod, RANK, 1)
         whole = jnp.where(lane < RANK, prod[:32], prod[32:])
-        for k in range(16):
-            g_own[k, 2 * d : 2 * d + 2] = whole[2 * k : 2 * k + 2]
+        for k in range(8):
+            g_own[k, SLICE * d : SLICE * (d + 1)] = whole[SLICE * k : SLICE * (k + 1)]
 
     g_copy = []
+    mine = pl.ds(pl.multiple_of(slot * 16, 16), 16)
     for peer in PEERS:
-        param = place(*peer)
-        g_copy.append(send(g_own.at[part(param)], g_all.at[pl.ds(pl.multiple_of(me * 8, 8), 8)], (doc, param)))
-    g_all[pl.ds(pl.multiple_of(me * 8, 8), 8), :] = g_own[part(me)]
+        g_copy.append(send(g_own.at[part(*peer)], g_all.at[mine], (doc, place(*peer, 0))))
+    g_all[mine, :] = g_own[part(0, 0)]
+
+    spread_twin()
+    for copy in t_twin:
+        copy.wait_recv()
+    for m in range(SLICE):
+        rows = jnp.stack([t_all[m, c].reshape(RANK, 8, 128) for c in (0, 1)], axis=1).reshape(1024, 128)
+        high, low = split(rows)
+        t_high[:, m * 128 : (m + 1) * 128] = high
+        t_low[:, m * 128 : (m + 1) * 128] = low
     for copy in g_copy:
         copy.wait_recv()
 
-    docs = jnp.concatenate([g_all[pl.ds(m, 64, stride=2), :] for m in (0, 1)], axis=1)
+    docs = jnp.concatenate([g_all[pl.ds(m, 32, stride=SLICE), :] for m in range(SLICE)], axis=1)
     high, low = split(docs)
     scores = dot(jnp.concatenate([high, low], axis=0), t_high[...], (1, 1))
-    scores = scores[:64] + scores[64:] + dot(high, t_low[...], (1, 1))
+    scores = scores[:32] + scores[32:] + dot(high, t_low[...], (1, 1))
     scores = scores * (1.0 / (RANK * SEQ**0.5))
-    for k in range(16):
+    for k in range(8):
         s_own[k] = scores[OWNED * k : OWNED * (k + 1)]
     s_copy = []
-    for peer in PEERS:
-        param = place(*peer)
-        s_copy.append(send(s_own.at[param], s_all.at[me], (doc, param)))
-    s_all[me] = s_own[me]
+    for dz, dy in PEERS:
+        param = place(dz, dy, 0)
+        s_copy.append(send(s_own.at[param // 2], s_all.at[slot], (doc, param)))
+    s_all[slot] = s_own[slot]
     for copy in s_copy:
         copy.wait_recv()
     total = s_all[0]
-    for k in range(1, 16):
+    for k in range(1, 8):
         total = total + s_all[k]
     out[...] = total
     for copy in sent:
@@ -375,13 +386,13 @@
             vmem((PART_A, 128), F32),
             vmem((4, ROWS - PART_A, 128), F32),
             vmem((32, 8, 128), F32),
-            vmem((2, 8, 16, 8, 128), F32),
-            vmem((1024, 256), BF16),
-            vmem((1024, 256), BF16),
-            vmem((16, 8, 128), F32),
+            vmem((SLICE, 2, 8, 8, 8, 128), F32),
+            vmem((1024, SLICE * 128), BF16),
+            vmem((1024, SLICE * 128), BF16),
+            vmem((8, SLICE * OWNED, 128), F32),
             vmem((128, 128), F32),
-            vmem((16, OWNED, 1024), F32),
-            vmem((16, OWNED, 1024), F32),
+            vmem((8, OWNED, 1024), F32),
+            vmem((8, OWNED, 1024), F32),
             pltpu.SemaphoreType.DMA((8, 2, 2)),
             pltpu.SemaphoreType.DMA((7,)),
             pltpu.SemaphoreType.DMA((N_SEMS,)),

time: 52.3 us -> 43.3 us (0.83)
  the two profiles are of different devices: /device:TPU:0 before, /device:TPU:1 now
where the time goes in v1:
time: 43.3 us; the launch traced here: 43.2 us
  Pallas kernels  41.8 us (97%)
  local copies, waits for them, and re-layouts  1.32 us (3%)
    pallas_call x1, Pallas kernels, body(): pl.pallas_call(kernel, out_shape=jax.ShapeDtypeStruct((OWNED, 1024), F32)...  41.8 us
    unnamed x1, local copies, waits for them, and re-layouts  1.32 us

profile of v1, /device:TPU:1, one launch (start us, length us, event | category | flops | bytes accessed | tf_op | source)
XLA Modules:
  0.0 43.2 jit_solution(2964200706992554220)
XLA Ops:
  0.0 41.8 %shard_map.91 = f32[4,1024]{1,0:T(4,128)} custom-call(bf16[64,864,128]{2,1,0:T(8,128)(2,1)} %bitcast.2, bf16[64,320,128]{2,1,0:T(8,128)(2,1)} %bitcast.3, bf16[64,864]{1,0:T(8,128)(2,1)} %pin.1, bf16[64,320]{1,0:T(8,128)(2,1)} %pout.1, s32[64]{0:T(128)} %lengths.1, s32[64,128]{1,0:T(8,128)} %mask.1, f32[8,4096]{1,0:T(8,128)} %queries.1, f32[64,64]{1,0:T(8,128)} %left.1, ...), custom_call_target="tpu_custom_call" | custom-call | flops 1300000000 | bytes 20000000 | tf_op jit(solution)/shard_map/pallas_call | solution.py:364
  41.8 1.3 %copy.11 = f32[4,1024]{1,0:T(4,128)} copy(f32[4,1024]{1,0:T(4,128)} %shard_map.91) | data formatting | bytes 32768

commit v2 on v1

--- a/solution.py
+++ b/solution.py
@@ -24,7 +24,8 @@
 PLACE = {step: j for j, step in enumerate(ORDER)}
 PEERS = ((2, 1), (2, 0), (1, 1), (3, 1), (1, 0), (3, 0), (0, 1))
 SLICE = 4
-N_SEMS = 8 + 18 + 5 + 7 + 2 + 4 + 3 + 7 + 7
+WIDE = SLICE * 128
+N_SEMS = 8 + 18 + 5 + 7 + 2 + 5 + 8 + 7 + 7
 
 
 def iota(shape, dim):
@@ -45,9 +46,9 @@
 def kernel(
     act, grad, pin, pout, lengths, mask, queries, left, right,
     out,
-    act_v, grad_v, pin_v, pout_v, len_s, mask_v, q_v, left_v, right_v, w_out,
+    act_v, grad_v, pin_v, pout_v, len_s, mask_v, left_v, right_v,
     blocks, twin, f_a, n_a, f_b, n_b, y_a, y_b,
-    t_own, t_all, t_high, t_low, g_own, g_all, s_own, s_all,
+    t_all, t_high, t_low, g_own, g_all, s_own, s_all,
     load_sem, small_sem, send_sem, recv_sem,
 ):
     doc, me = lax.axis_index("doc"), lax.axis_index("param")
@@ -76,16 +77,15 @@
         pltpu.make_async_copy(src, dst, small_sem.at[i])
         for i, (src, dst) in enumerate(
             (
-                (pin, pin_v), (pout, pout_v), (queries, q_v), (left, left_v), (right, right_v),
-                (mask, mask_v), (lengths, len_s),
+                (pout, pout_v), (pin, pin_v), (left, left_v), (right, right_v), (mask, mask_v), (lengths, len_s),
             )
         )
     ]
-    for copy in small[:5]:
+    for copy in small[:2]:
         copy.start()
     for copy in loads(0):
         copy.start()
-    for copy in small[5:]:
+    for copy in small[2:]:
         copy.start()
     for j in range(1, AHEAD):
         for copy in loads(j):
@@ -98,13 +98,6 @@
     greet.append(y_next)
     for device in greet:
         pl.semaphore_signal(barrier, inc=1, device_id=device, device_id_type=MESH)
-
-    small[0].wait()
-    small[1].wait()
-    r_, c_ = iota((RANK, RANK), 0), iota((RANK, RANK), 1)
-    odd = (r_ >= 32).astype(jnp.int32)
-    pick = jnp.where(c_ == 2 * (r_ - 32 * odd) + odd, 1.0, 0.0).astype(BF16)
-    w_out[...] = dot(pick, pout_v[...]).astype(BF16)
 
     counter = [0]
     sent = []
@@ -125,21 +118,21 @@
     core_copy, y_copy, z_copy = {}, {}, {}
 
     def project(j):
-        for copy in loads(j):
-            copy.wait()
-
-        def one(i, carry):
-            r = 1 - i
+        copies = loads(j)
+
+        def one(r):
+            for copy in copies[:2] if r else copies[2:]:
+                copy.wait()
             a = jnp.concatenate([act_v[j, r, d] for d in range(OWNED)], axis=1)
             g = jnp.concatenate([grad_v[j, r, d] for d in range(OWNED)], axis=1)
-            o_rows, i_rows = dot(w_out[...], g), dot(pin_v[...], a)
+            o_rows, i_rows = dot(pout_v[...], g), dot(pin_v[...], a)
             for d in range(OWNED):
                 blocks[j, r, d * SEQ : d * SEQ + RANK] = o_rows[:, d * SEQ : (d + 1) * SEQ]
                 blocks[j, r, d * SEQ + RANK : (d + 1) * SEQ] = i_rows[:, d * SEQ : (d + 1) * SEQ]
-            return carry
-
-        lax.fori_loop(0, 2, one, 0)
+
+        one(1)
         core_copy[j] = send(blocks.at[j, 1], twin.at[j], twin_id)
+        one(0)
 
     def ref(t, dz, half):
         if t < 2:
@@ -195,65 +188,61 @@
         y_copy[dz].wait_recv()
         blocks[PLACE[dz, 1], 0, PART_A:ROWS] += y_b[dz]
 
-    def precondition():
-        for copy in small[2:5]:
-            copy.wait()
-        pick32 = pick.astype(F32)
-        l_perm = dot(dot(pick32, left_v[...], precision=HIGHEST), pick32, (1, 1), precision=HIGHEST)
-        none = jnp.zeros((RANK, RANK), F32)
-        r_twice = jnp.concatenate(
-            [jnp.concatenate([right_v[...], none], axis=1), jnp.concatenate([none, right_v[...]], axis=1)], axis=0
-        )
-        rows = jnp.concatenate([q_v[:, m * 128 : (m + 1) * 128] for m in range(32)], axis=0)
-        t_own[...] = dot(rows, r_twice, precision=HIGHEST).reshape(32, 8, 128)
-        lane = iota((32, 128), 1) < RANK
-
-        def pair(a, b):
-            return jnp.where(lane, a, pltpu.roll(b, RANK, 1)), jnp.where(lane, pltpu.roll(a, RANK, 1), b)
-
-        pairs = [pair(t_own[:, 2 * i], t_own[:, 2 * i + 1]) for i in range(4)]
-        cols = jnp.concatenate([jnp.concatenate(p, axis=0) for p in pairs], axis=1)
-        cols = dot(l_perm, cols, precision=HIGHEST)
-        for i in range(4):
-            a, b = pair(cols[:32, i * 128 : (i + 1) * 128], cols[32:, i * 128 : (i + 1) * 128])
-            t_own[:, 2 * i] = a
-            t_own[:, 2 * i + 1] = b
-
     slot = me // 2
-    t_copy, t_twin = [], []
-
-    def share(first, count):
-        block = t_all.at[:, core, pl.ds(first, count)]
-        t_twin.append(send(block, block, twin_id))
+    t_copy, t_twin, t_y, t_x = [], [], [], {}
+
+    def piece(k):
+        return queries.at[:, pl.ds(pl.multiple_of(WIDE * k, WIDE), WIDE)]
+
+    own_piece = pltpu.make_async_copy(piece(part(0, 0)), t_all.at[core, doc, slot], small_sem.at[len(small)])
+
+    def spread(g, device):
+        block = t_all.at[core, g]
+        return send(block, block, device)
+
+    def share(g):
+        t_twin.append(spread(g, twin_id))
+
+    def x_id(dx):
+        return (lax.rem(x + dx, 4) * 2 + hi, me)
+
+    def x_doc(dx, half):
+        return 2 * lax.rem(x + 4 - dx, 4) + (1 - hi if half else hi)
 
     def spread_queries():
+        own_piece.start()
         for peer in PEERS:
-            t_copy.append(
-                send(
-                    t_own.at[pl.ds(SLICE * part(*peer), SLICE)], t_all.at[:, core, doc, slot], (doc, place(*peer, 0))
-                )
-            )
-        mine = part(0, 0)
-        for m in range(SLICE):
-            t_all[m, core, doc, slot] = t_own[SLICE * mine + m]
-
-    def spread_y():
+            t_copy.append(send(piece(part(*peer)), t_all.at[core, doc, slot], (doc, place(*peer, 0))))
+
+    def spread_own():
+        own_piece.wait()
         for copy in t_copy:
             copy.wait_recv()
-        t_copy.append(send(t_all.at[:, core, doc], t_all.at[:, core, doc], y_next))
-
-    def spread_x():
-        t_copy.pop().wait_recv()
-        t_copy.clear()
-        block = t_all.at[:, core, pl.ds(2 * x, 2)]
+        t_y.append(spread(doc, y_next))
         for dx in (2, 1, 3):
-            t_copy.append(send(block, block, (lax.rem(x + dx, 4) * 2 + hi, me)))
-        share(2 * x, 2)
-
-    def spread_twin():
-        for dx, copy in zip((1, 3, 2), (t_copy[1], t_copy[2], t_copy[0])):
-            copy.wait_recv()
-            share(2 * lax.rem(x + 4 - dx, 4), 2)
+            t_x[dx, 0] = spread(doc, x_id(dx))
+        share(doc)
+
+    def spread_other():
+        t_y[0].wait_recv()
+        for dx in (1, 3):
+            t_x[dx, 1] = spread(x_doc(0, 1), x_id(dx))
+        share(x_doc(0, 1))
+
+    def spread_far():
+        t_x[2, 0].wait_recv()
+        t_y.append(spread(x_doc(2, 0), y_next))
+        share(x_doc(2, 0))
+
+    def spread_twin(half):
+        for dx in (1, 3):
+            t_x[dx, half].wait_recv()
+            share(x_doc(dx, half))
+
+    def spread_last():
+        spread_twin(1)
+        t_y[1].wait_recv()
+        share(x_doc(2, 1))
 
     def chunk(j):
         if j + AHEAD < len(ORDER):
@@ -261,9 +250,10 @@
                 copy.start()
         project(j)
 
-    precondition()
     pl.semaphore_wait(barrier, len(greet))
     spread_queries()
+    for copy in small[:2]:
+        copy.wait()
     chunk(0)
     chunk(1)
     collect(0)
@@ -271,52 +261,74 @@
     collect(1)
     chunk(3)
     collect(2)
-    spread_y()
+    spread_own()
     chunk(4)
     collect(3)
     send_up_sum(0)
     chunk(5)
     collect(4)
     send_down_sum(0)
+    y_sum(2)
+    send_far(2)
     chunk(6)
     collect(5)
     send_up_sum(1)
     send_down_sum(1)
     chunk(7)
     collect(6)
-    y_sum(2)
-    send_far(2)
     collect(7)
-    spread_x()
+    spread_other()
     y_sum(1)
     send_up_now(2)
+    finish(0)
+    last = send(blocks.at[PLACE[0, 0], 0, pl.ds(0, PART_A)], y_a, y_id)
+    spread_far()
     y_sum(3)
     send_down_now(2)
-    finish(0)
-    last = send(blocks.at[PLACE[0, 0], 0, pl.ds(0, PART_A)], y_a, y_id)
+    spread_twin(0)
     send_up_sum(2)
     send_down_sum(2)
     finish(1)
+    for copy in small[2:]:
+        copy.wait()
+    r_, c_ = iota((RANK, RANK), 0), iota((RANK, RANK), 1)
+    odd = (r_ >= 32).astype(jnp.int32)
+    pick = jnp.where(c_ == 2 * (r_ - 32 * odd) + odd, 1.0, 0.0)
+    none = jnp.zeros((RANK, RANK), F32)
+    p_high, p_low = split(
+        jnp.concatenate(
+            [
+                jnp.concatenate([dot(pick, left_v[...], (1, 1), precision=HIGHEST), none], axis=1),
+                jnp.concatenate([none, right_v[...]], axis=1),
+            ],
+            axis=0,
+        )
+    )
+    home = PLACE[0, 1]
+    lane = iota((32, 128), 1)
+
+    def gradients(docs):
+        cols = jnp.concatenate([blocks[home, 0, d * SEQ : (d + 1) * SEQ] for d in docs], axis=1)
+        high, low = split(cols)
+        cols = dot(p_high, high) + (dot(p_high, low) + dot(p_low, high))
+        for i, d in enumerate(docs):
+            row = me * OWNED + d
+            weight = jnp.where(iota((1, SEQ), 1) < len_s[row], mask_v[pl.ds(row, 1), :].astype(F32), 0.0)
+            o_rows = cols[:RANK, i * SEQ : (i + 1) * SEQ] * weight
+            i_rows = cols[RANK:, i * SEQ : (i + 1) * SEQ]
+            prod = dot(jnp.concatenate(split(o_rows), axis=0), jnp.concatenate(split(i_rows), axis=0), (1, 1))
+            prod = prod[:RANK] + prod[RANK:]
+            prod = prod + pltpu.roll(prod, RANK, 1)
+            whole = jnp.where(lane < RANK, prod[:32], prod[32:])
+            for k in range(8):
+                g_own[k, SLICE * d : SLICE * (d + 1)] = whole[SLICE * k : SLICE * (k + 1)]
+
+    last.wait_recv()
+    blocks[home, 0, 0:PART_A] += y_a[...]
+    gradients((0, 1))
     y_sum(0)
     finish(2)
-    last.wait_recv()
-    home = PLACE[0, 1]
-    blocks[home, 0, 0:PART_A] += y_a[...]
-
-    for copy in small[5:]:
-        copy.wait()
-    lane = iota((32, 128), 1)
-    for d in range(OWNED):
-        row = me * OWNED + d
-        weight = jnp.where(iota((1, SEQ), 1) < len_s[row], mask_v[pl.ds(row, 1), :].astype(F32), 0.0)
-        o_rows = blocks[home, 0, d * SEQ : d * SEQ + RANK] * weight
-        i_rows = blocks[home, 0, d * SEQ + RANK : (d + 1) * SEQ]
-        prod = dot(jnp.concatenate(split(o_rows), axis=0), jnp.concatenate(split(i_rows), axis=0), (1, 1))
-        prod = prod[:RANK] + prod[RANK:]
-        prod = prod + pltpu.roll(prod, RANK, 1)
-        whole = jnp.where(lane < RANK, prod[:32], prod[32:])
-        for k in range(8):
-            g_own[k, SLICE * d : SLICE * (d + 1)] = whole[SLICE * k : SLICE * (k + 1)]
+    gradients((2, 3))
 
     g_copy = []
     mine = pl.ds(pl.multiple_of(slot * 16, 16), 16)
@@ -324,14 +336,14 @@
         g_copy.append(send(g_own.at[part(*peer)], g_all.at[mine], (doc, place(*peer, 0))))
     g_all[mine, :] = g_own[part(0, 0)]
 
-    spread_twin()
+    spread_last()
     for copy in t_twin:
         copy.wait_recv()
-    for m in range(SLICE):
-        rows = jnp.stack([t_all[m, c].reshape(RANK, 8, 128) for c in (0, 1)], axis=1).reshape(1024, 128)
-        high, low = split(rows)
-        t_high[:, m * 128 : (m + 1) * 128] = high
-        t_low[:, m * 128 : (m + 1) * 128] = low
+    rows = jnp.stack([t_all[c].reshape(RANK, 8, WIDE) for c in (0, 1)], axis=1).reshape(1024, WIDE)
+    t_high[...], t_low[...] = split(rows)
+    early = [copy for copy in sent if not any(copy is other for other in g_copy)]
+    for copy in early:
+        copy.wait_send()
     for copy in g_copy:
         copy.wait_recv()
 
@@ -353,7 +365,7 @@
     for k in range(1, 8):
         total = total + s_all[k]
     out[...] = total
-    for copy in sent:
+    for copy in g_copy + s_copy:
         copy.wait_send()
 
 
@@ -373,10 +385,8 @@
             vmem(proj_out.shape, BF16),
             pltpu.SMEM(lengths.shape, jnp.int32),
             vmem(loss_mask.shape, jnp.int32),
-            vmem(queries.shape, F32),
             vmem(left_pre.shape, F32),
             vmem(right_pre.shape, F32),
-            vmem(proj_out.shape, BF16),
             vmem((8, 2, ROWS, 128), F32),
             vmem((8, ROWS, 128), F32),
             vmem((2, 2, HALF_A, 128), F32),
@@ -385,10 +395,9 @@
             vmem((2, 2, HALF_B, 128), F32),
             vmem((PART_A, 128), F32),
             vmem((4, ROWS - PART_A, 128), F32),
-            vmem((32, 8, 128), F32),
-            vmem((SLICE, 2, 8, 8, 8, 128), F32),
-            vmem((1024, SLICE * 128), BF16),
-            vmem((1024, SLICE * 128), BF16),
+            vmem((2, 8, 8, 8, WIDE), F32),
+            vmem((1024, WIDE), BF16),
+            vmem((1024, WIDE), BF16),
             vmem((8, SLICE * OWNED, 128), F32),
             vmem((128, 128), F32),
             vmem((8, OWNED, 1024), F32),

time: 43.3 us -> 36.4 us (0.84)
  the two profiles are of different devices: /device:TPU:1 before, /device:TPU:0 now
where the time goes in v2:
time: 36.4 us; the launch traced here: 36.2 us
  Pallas kernels  34.9 us (96%)
  local copies, waits for them, and re-layouts  1.32 us (4%)
    pallas_call x1, Pallas kernels, body(): pl.pallas_call(kernel, out_shape=jax.ShapeDtypeStruct((OWNED, 1024), F32)...  34.9 us
    unnamed x1, local copies, waits for them, and re-layouts  1.32 us

profile of v2, /device:TPU:0, one launch (start us, length us, event | category | flops | bytes accessed | tf_op | source)
XLA Modules:
  0.0 36.2 jit_solution(9337814146799621373)
XLA Ops:
  0.0 34.9 %shard_map.91 = f32[4,1024]{1,0:T(4,128)} custom-call(bf16[64,864,128]{2,1,0:T(8,128)(2,1)} %bitcast.2, bf16[64,320,128]{2,1,0:T(8,128)(2,1)} %bitcast.3, bf16[64,864]{1,0:T(8,128)(2,1)} %pin.1, bf16[64,320]{1,0:T(8,128)(2,1)} %pout.1, s32[64]{0:T(128)} %lengths.1, s32[64,128]{1,0:T(8,128)} %mask.1, f32[8,4096]{1,0:T(8,128)} %queries.1, f32[64,64]{1,0:T(8,128)} %left.1, ...), custom_call_target="tpu_custom_call" | custom-call | flops 1300000000 | bytes 20000000 | tf_op jit(solution)/shard_map/pallas_call | solution.py:376
  34.9 1.3 %copy.11 = f32[4,1024]{1,0:T(4,128)} copy(f32[4,1024]{1,0:T(4,128)} %shard_map.91) | data formatting | bytes 32768

commit v3 on v2

--- a/solution.py
+++ b/solution.py
@@ -66,11 +66,11 @@
 
     def loads(j):
         dz, own = ORDER[j]
-        found = []
-        for r in (1, 0):
-            first = place(dz, 1 - own, r) * OWNED
-            found.append(pltpu.make_async_copy(act.at[pl.ds(first, OWNED)], act_v.at[j, r], load_sem.at[j, r, 0]))
-            found.append(pltpu.make_async_copy(grad.at[pl.ds(first, OWNED)], grad_v.at[j, r], load_sem.at[j, r, 1]))
+        first = place(dz, 1 - own, 0) // 2 * 2 * OWNED
+        found = [
+            pltpu.make_async_copy(act.at[pl.ds(first, 2 * OWNED)], act_v.at[j], load_sem.at[j, 0]),
+            pltpu.make_async_copy(grad.at[pl.ds(first, 2 * OWNED)], grad_v.at[j], load_sem.at[j, 1]),
+        ]
         return found
 
     small = [
@@ -118,13 +118,13 @@
     core_copy, y_copy, z_copy = {}, {}, {}
 
     def project(j):
-        copies = loads(j)
+        for copy in loads(j):
+            copy.wait()
 
         def one(r):
-            for copy in copies[:2] if r else copies[2:]:
-                copy.wait()
-            a = jnp.concatenate([act_v[j, r, d] for d in range(OWNED)], axis=1)
-            g = jnp.concatenate([grad_v[j, r, d] for d in range(OWNED)], axis=1)
+            docs = (1 - core if r else core) * OWNED
+            a = jnp.concatenate([act_v[j, docs + d] for d in range(OWNED)], axis=1)
+            g = jnp.concatenate([grad_v[j, docs + d] for d in range(OWNED)], axis=1)
             o_rows, i_rows = dot(pout_v[...], g), dot(pin_v[...], a)
             for d in range(OWNED):
                 blocks[j, r, d * SEQ : d * SEQ + RANK] = o_rows[:, d * SEQ : (d + 1) * SEQ]
@@ -351,7 +351,6 @@
     high, low = split(docs)
     scores = dot(jnp.concatenate([high, low], axis=0), t_high[...], (1, 1))
     scores = scores[:32] + scores[32:] + dot(high, t_low[...], (1, 1))
-    scores = scores * (1.0 / (RANK * SEQ**0.5))
     for k in range(8):
         s_own[k] = scores[OWNED * k : OWNED * (k + 1)]
     s_copy = []
@@ -375,12 +374,12 @@
     vmem = pltpu.VMEM
     return pl.pallas_call(
         kernel,
-        out_shape=jax.ShapeDtypeStruct((OWNED, 1024), F32),
+        out_shape=pltpu.VMEM((OWNED, 1024), F32),
         in_specs=[pl.BlockSpec(memory_space=pl.ANY)] * 9,
         out_specs=pl.BlockSpec(memory_space=pltpu.VMEM),
         scratch_shapes=[
-            vmem((8, 2, OWNED, wide_in, SEQ), BF16),
-            vmem((8, 2, OWNED, wide_out, SEQ), BF16),
+            vmem((8, 2 * OWNED, wide_in, SEQ), BF16),
+            vmem((8, 2 * OWNED, wide_out, SEQ), BF16),
             vmem(proj_in.shape, BF16),
             vmem(proj_out.shape, BF16),
             pltpu.SMEM(lengths.shape, jnp.int32),
@@ -402,7 +401,7 @@
             vmem((128, 128), F32),
             vmem((8, OWNED, 1024), F32),
             vmem((8, OWNED, 1024), F32),
-            pltpu.SemaphoreType.DMA((8, 2, 2)),
+            pltpu.SemaphoreType.DMA((8, 2)),
             pltpu.SemaphoreType.DMA((7,)),
             pltpu.SemaphoreType.DMA((N_SEMS,)),
             pltpu.SemaphoreType.DMA((N_SEMS,)),
@@ -411,7 +410,7 @@
             collective_id=0, has_side_effects=True, vmem_limit_bytes=60 * 1024 * 1024
         ),
         cost_estimate=pl.CostEstimate(flops=1_300_000_000, bytes_accessed=20_000_000, transcendentals=0),
-    )(activations, out_grads, proj_in, proj_out, lengths, loss_mask, queries, left_pre, right_pre)
+    )(activations, out_grads, proj_in, proj_out, lengths, loss_mask, queries, left_pre, right_pre) * (1.0 / (RANK * SEQ**0.5))
 
 
 def solution(mesh):

time: 36.4 us -> 34.9 us (0.959)
  local copies, waits for them, and re-layouts: 1.32 us -> 0 us
  Pallas kernels: 34.9 us -> 34.1 us
  other arithmetic: 0 us -> 0.61 us
    unnamed x1 -> x0, local copies, waits for them, and re-layouts: 1.32 us -> none
    pallas_call x1, Pallas kernels: 34.9 us -> 34.1 us  [body(): pl.pallas_call(kernel, out_shape=pltpu.VMEM((OWNED, 1024), F32), in_specs...]
    mul x0 -> x1, other arithmetic: none -> 0.61 us  [body(): pl.pallas_call(kernel, out_shape=pltpu.VMEM((OWNED, 1024), F32), in_specs...]
where the time goes in v3:
time: 34.9 us; the launch traced here: 34.8 us
  Pallas kernels  34.1 us (98%)
  other arithmetic  0.61 us (2%)
    pallas_call x1, Pallas kernels, body(): pl.pallas_call(kernel, out_shape=pltpu.VMEM((OWNED, 1024), F32), in_specs...  34.1 us

profile of v3, /device:TPU:0, one launch (start us, length us, event | category | flops | bytes accessed | tf_op | source)
XLA Modules:
  0.0 34.8 jit_solution(4342058349029910603)
XLA Ops:
  0.0 34.1 %shard_map.91 = f32[4,1024]{1,0:T(4,128)S(1)} custom-call(bf16[64,864,128]{2,1,0:T(8,128)(2,1)} %bitcast.2, bf16[64,320,128]{2,1,0:T(8,128)(2,1)} %bitcast.3, bf16[64,864]{1,0:T(8,128)(2,1)} %pin.1, bf16[64,320]{1,0:T(8,128)(2,1)} %pout.1, s32[64]{0:T(128)} %lengths.1, s32[64,128]{1,0:T(8,128)} %mask.1, f32[8,4096]{1,0:T(8,128)} %queries.1, f32[64,64]{1,0:T(8,128)} %left.1, ...), custom_call_target="tpu_custom_call" | custom-call | flops 1300000000 | bytes 20000000 | tf_op jit(solution)/shard_map/pallas_call | solution.py:375
  34.1 0.6 %broadcast_multiply_fusion = f32[4,1024]{1,0:T(4,128)} fusion(f32[4,1024]{1,0:T(4,128)S(1)} %shard_map.91), kind=kLoop, calls=%fused_computation | loop fusion | flops 4096 | bytes 32768 | tf_op jit(solution)/shard_map/mul | solution.py:375

commit v4 on v3

--- a/solution.py
+++ b/solution.py
@@ -73,6 +73,14 @@
         ]
         return found
 
+    barrier = pltpu.get_barrier_semaphore()
+    greet = [(doc, place(*peer, 0)) for peer in PEERS] + [(doc, place(0, 0, 1))]
+    greet += [(lax.rem(x + dx, 4) * 2 + hi, me) for dx in (1, 2, 3)]
+    y_next = (x * 2 + 1 - hi, place(0, 1, 0))
+    greet.append(y_next)
+    for device in greet:
+        pl.semaphore_signal(barrier, inc=1, device_id=device, device_id_type=MESH)
+
     small = [
         pltpu.make_async_copy(src, dst, small_sem.at[i])
         for i, (src, dst) in enumerate(
@@ -81,23 +89,11 @@
             )
         )
     ]
-    for copy in small[:2]:
-        copy.start()
-    for copy in loads(0):
-        copy.start()
-    for copy in small[2:]:
+    for copy in loads(0) + small:
         copy.start()
     for j in range(1, AHEAD):
         for copy in loads(j):
             copy.start()
-
-    barrier = pltpu.get_barrier_semaphore()
-    greet = [(doc, place(*peer, 0)) for peer in PEERS] + [(doc, place(0, 0, 1))]
-    greet += [(lax.rem(x + dx, 4) * 2 + hi, me) for dx in (1, 2, 3)]
-    y_next = (x * 2 + 1 - hi, place(0, 1, 0))
-    greet.append(y_next)
-    for device in greet:
-        pl.semaphore_signal(barrier, inc=1, device_id=device, device_id_type=MESH)
 
     counter = [0]
     sent = []
@@ -336,14 +332,16 @@
         g_copy.append(send(g_own.at[part(*peer)], g_all.at[mine], (doc, place(*peer, 0))))
     g_all[mine, :] = g_own[part(0, 0)]
 
+    done = len(sent)
+    for copy in sent[:done]:
+        copy.wait_send()
     spread_last()
+    for copy in sent[done:]:
+        copy.wait_send()
     for copy in t_twin:
         copy.wait_recv()
     rows = jnp.stack([t_all[c].reshape(RANK, 8, WIDE) for c in (0, 1)], axis=1).reshape(1024, WIDE)
     t_high[...], t_low[...] = split(rows)
-    early = [copy for copy in sent if not any(copy is other for other in g_copy)]
-    for copy in early:
-        copy.wait_send()
     for copy in g_copy:
         copy.wait_recv()
 
@@ -359,13 +357,13 @@
         s_copy.append(send(s_own.at[param // 2], s_all.at[slot], (doc, param)))
     s_all[slot] = s_own[slot]
     for copy in s_copy:
+        copy.wait_send()
+    for copy in s_copy:
         copy.wait_recv()
     total = s_all[0]
     for k in range(1, 8):
         total = total + s_all[k]
     out[...] = total
-    for copy in g_copy + s_copy:
-        copy.wait_send()
 
 
 def body(activations, out_grads, proj_in, proj_out, lengths, loss_mask, queries, left_pre, right_pre):
@@ -398,7 +396,7 @@
             vmem((1024, WIDE), BF16),
             vmem((1024, WIDE), BF16),
             vmem((8, SLICE * OWNED, 128), F32),
-            vmem((128, 128), F32),
+            vmem((136, 128), F32),
             vmem((8, OWNED, 1024), F32),
             vmem((8, OWNED, 1024), F32),
             pltpu.SemaphoreType.DMA((8, 2)),

time: 34.9 us -> 34.8 us (level)
  no operation moved by 1% of the time
where the time goes in v4:
time: 34.8 us; the launch traced here: 34.7 us
  Pallas kernels  34 us (98%)
  other arithmetic  0.61 us (2%)
    pallas_call x1, Pallas kernels, body(): pl.pallas_call(kernel, out_shape=pltpu.VMEM((OWNED, 1024), F32), in_specs...  34 us

profile of v4, /device:TPU:0, one launch (start us, length us, event | category | flops | bytes accessed | tf_op | source)
XLA Modules:
  0.0 34.7 jit_solution(8068843133567693465)
XLA Ops:
  0.0 34.0 %shard_map.91 = f32[4,1024]{1,0:T(4,128)S(1)} custom-call(bf16[64,864,128]{2,1,0:T(8,128)(2,1)} %bitcast.2, bf16[64,320,128]{2,1,0:T(8,128)(2,1)} %bitcast.3, bf16[64,864]{1,0:T(8,128)(2,1)} %pin.1, bf16[64,320]{1,0:T(8,128)(2,1)} %pout.1, s32[64]{0:T(128)} %lengths.1, s32[64,128]{1,0:T(8,128)} %mask.1, f32[8,4096]{1,0:T(8,128)} %queries.1, f32[64,64]{1,0:T(8,128)} %left.1, ...), custom_call_target="tpu_custom_call" | custom-call | flops 1300000000 | bytes 20000000 | tf_op jit(solution)/shard_map/pallas_call | solution.py:373
  34.1 0.6 %broadcast_multiply_fusion = f32[4,1024]{1,0:T(4,128)} fusion(f32[4,1024]{1,0:T(4,128)S(1)} %shard_map.91), kind=kLoop, calls=%fused_computation | loop fusion | flops 4096 | bytes 32768 | tf_op jit(solution)/shard_map/mul | solution.py:373

commit v5 on v4

--- a/solution.py
+++ b/solution.py
@@ -260,12 +260,12 @@
     spread_own()
     chunk(4)
     collect(3)
+    y_sum(2)
+    send_far(2)
     send_up_sum(0)
+    send_down_sum(0)
     chunk(5)
     collect(4)
-    send_down_sum(0)
-    y_sum(2)
-    send_far(2)
     chunk(6)
     collect(5)
     send_up_sum(1)
@@ -278,12 +278,12 @@
     send_up_now(2)
     finish(0)
     last = send(blocks.at[PLACE[0, 0], 0, pl.ds(0, PART_A)], y_a, y_id)
-    spread_far()
     y_sum(3)
     send_down_now(2)
-    spread_twin(0)
     send_up_sum(2)
     send_down_sum(2)
+    spread_far()
+    spread_twin(0)
     finish(1)
     for copy in small[2:]:
         copy.wait()

time: 34.8 us -> 34.8 us (level)
  no operation moved by 1% of the time
where the time goes in v5:
time: 34.8 us; the launch traced here: 34.7 us
  Pallas kernels  34.1 us (98%)
  other arithmetic  0.61 us (2%)
    pallas_call x1, Pallas kernels, body(): pl.pallas_call(kernel, out_shape=pltpu.VMEM((OWNED, 1024), F32), in_specs...  34.1 us

profile of v5, /device:TPU:0, one launch (start us, length us, event | category | flops | bytes accessed | tf_op | source)
XLA Modules:
  0.0 34.7 jit_solution(2243445689868736516)
XLA Ops:
  0.0 34.1 %shard_map.91 = f32[4,1024]{1,0:T(4,128)S(1)} custom-call(bf16[64,864,128]{2,1,0:T(8,128)(2,1)} %bitcast.2, bf16[64,320,128]{2,1,0:T(8,128)(2,1)} %bitcast.3, bf16[64,864]{1,0:T(8,128)(2,1)} %pin.1, bf16[64,320]{1,0:T(8,128)(2,1)} %pout.1, s32[64]{0:T(128)} %lengths.1, s32[64,128]{1,0:T(8,128)} %mask.1, f32[8,4096]{1,0:T(8,128)} %queries.1, f32[64,64]{1,0:T(8,128)} %left.1, ...), custom_call_target="tpu_custom_call" | custom-call | flops 1300000000 | bytes 20000000 | tf_op jit(solution)/shard_map/pallas_call | solution.py:373
  34.1 0.6 %broadcast_multiply_fusion = f32[4,1024]{1,0:T(4,128)} fusion(f32[4,1024]{1,0:T(4,128)S(1)} %shard_map.91), kind=kLoop, calls=%fused_computation | loop fusion | flops 4096 | bytes 32768 | tf_op jit(solution)/shard_map/mul | solution.py:373
